TPU v7x, 128 devices: a whole 4x4x4 slice. The times are simulated.
128 devices in a mesh: tile: 16 (over y, z), plane: 8 (over x, core).
Axes of the slice: x: 4, y: 4, z: 4, core: 2. Of those that a mesh axis runs over, the one named last changes fastest.
Arguments:
- reference_image: bfloat16 [512, 4096], P('plane', 'tile'), may hold values from -6 to 6
- source_images: bfloat16 [6, 512, 4096], P(None, 'plane', 'tile'), may hold values from -6 to 6
- warps: bfloat16 [6, 32, 4, 256, 4096], P(None, 'plane', None, None, 'tile'), may hold values from -0.1875 to 0.1875
- offsets: int32 [6, 32, 4, 16], P(None, 'plane', None, 'tile'), may hold values from -1 to 1
Outputs:
- cost_volume: float32 [32, 512, 4096], P('plane', None, 'tile')
- best_cost: float32 [512, 4096], P('plane', 'tile')
All inputs are finite; a program needn't handle non-finite values.
Results may differ from a plain program's by a relative error of at most 0.0005.
Values may be sent and summed in bfloat16 or wider, within the bound.
A program may use at most 192 MiB of HBM per device.

v0:
```python
import jax
import jax.numpy as jnp
from jax import lax
from jax.sharding import PartitionSpec as P

HALF = 3


stabilizer = 4.0


def extended_2(cells, sides, width):
    for axis, dim in sides:
        count = lax.axis_size(axis)
        ends = count - 1
        head = lax.slice_in_dim(cells, 0, width, axis=dim)
        tail = lax.slice_in_dim(cells, cells.shape[dim] - width, cells.shape[dim], axis=dim)
        cells = jnp.concatenate(
            [
                lax.ppermute(tail, axis, [(i, (i + 1) % count) for i in range(ends)]),
                cells,
                lax.ppermute(head, axis, [((i + 1) % count, i) for i in range(ends)]),
            ],
            axis=dim,
        )
    return cells


def row_box(values):
    height = values.shape[-2]
    padded = jnp.pad(values, ((0, 0), (HALF, HALF), (0, 0)))
    rowed = padded[:, 0:height, :]
    for offset_row in range(1, 2 * HALF + 1):
        rowed = rowed + padded[:, offset_row : offset_row + height, :]
    return rowed


def column_box(extended):
    width_tile = extended.shape[-1] - 2 * HALF
    summed = extended[..., 0:width_tile]
    for offset_col in range(1, 2 * HALF + 1):
        summed = summed + extended[..., offset_col : offset_col + width_tile]
    return summed


def correlation(sum_r, sum_rr, sum_w, sum_ww, sum_rw):
    count = float((2 * HALF + 1) ** 2)
    covar = sum_rw - sum_r * sum_w / count
    var_ref = sum_rr - sum_r * sum_r / count
    var_warp = sum_ww - sum_w * sum_w / count
    return covar * lax.rsqrt((var_ref + stabilizer) * (var_warp + stabilizer))


def warp_plane(wide_src, shifts, matrices):
    view_count, slot_count, tile_width, _ = matrices.shape
    positions = jnp.arange(3, dtype=jnp.int32)
    picks = (shifts[:, :, None] + 1 == positions[None, None, :]).astype(jnp.bfloat16)
    placed = (picks[:, :, :, None, None] * matrices[:, :, None, :, :]).reshape(
        view_count, slot_count, 3 * tile_width, tile_width
    )
    terms = jnp.einsum("vrk,vskt->vsrt", wide_src, placed, preferred_element_type=jnp.float32)
    return jnp.sum(terms, axis=1)


def local(reference_image, source_images, warps, offsets):
    tile_width = warps.shape[-1]
    full_ref, full_src = (
        lax.all_gather(reference_image, "plane", axis=0, tiled=True),
        lax.all_gather(source_images, "plane", axis=1, tiled=True),
    )
    wide_src = extended_2(full_src, (("tile", 2),), tile_width)
    ref_float = full_ref.astype(jnp.float32)
    view_count = source_images.shape[0]
    local_planes = warps.shape[1]
    plane_costs = []
    ref_rows = row_box(jnp.stack([ref_float, ref_float * ref_float]))
    ref_sums = column_box(
        extended_2(ref_rows.astype(jnp.bfloat16), (("tile", 2),), HALF).astype(ref_rows.dtype)
    )
    for plane_local in range(local_planes):
        warped = warp_plane(wide_src, offsets[:, plane_local, :, 0], warps[:, plane_local])
        warp_stats = jnp.concatenate([warped, warped * warped, ref_float[None] * warped], axis=0)
        stat_rows = row_box(warp_stats)
        box_sums = column_box(
            extended_2(stat_rows.astype(jnp.bfloat16), (("tile", 2),), HALF).astype(stat_rows.dtype)
        )
        normalized = correlation(
            ref_sums[0][None],
            ref_sums[1][None],
            box_sums[0:view_count],
            box_sums[view_count : 2 * view_count],
            box_sums[2 * view_count :],
        )
        plane_costs.append(jnp.sum(1.0 - normalized, axis=0) / view_count)
    volume = jnp.stack(plane_costs)
    lowest = jnp.min(volume, axis=0)
    plane_count = lax.axis_size("plane")
    part_rows = lowest.shape[0] // plane_count
    everywhere = lax.pmin(lowest, "plane")
    best_cost = lax.dynamic_slice_in_dim(
        everywhere, lax.axis_index("plane") * part_rows, part_rows, 0
    )
    return (volume, best_cost)


def solution(mesh):
    return jax.shard_map(
        local,
        mesh=mesh,
        in_specs=(
            P("plane", "tile"),
            P(None, "plane", "tile"),
            P(None, "plane", None, None, "tile"),
            P(None, "plane", None, "tile"),
        ),
        out_specs=(P("plane", None, "tile"), P("plane", "tile")),
        check_vma=False,
    )
```

profile of v0, /device:TPU:1, one launch (start us, length us, event | category | flops | bytes accessed | tf_op | source)
XLA Modules:
  0.0 612.4 jit_solution(16470708076596417403)
XLA Ops:
  7.9 14.7 %all_gather.7 = bf16[512,256]{1,0:T(8,128)(2,1)S(1)} all-gather(bf16[64,256]{1,0:T(8,128)(2,1)} %param.4), channel_id=1, replica_groups=mesh['tile'=16,'plane'=8] {'plane'}, dimensions={0}, use_global_device_ids=true | all-gather | bytes 294912 | tf_op jit(solution)/shard_map/all_gather | solution.py:68
  23.6 3.6 collective-permute-start.4
  27.2 1.3 collective-permute-start.5
  29.5 8.3 %all-gather.2.cloned.1.call-done = bf16[6,512,256]{2,1,0:T(8,128)(2,1)} async-done(((bf16[6,64,256]{2,1,0:T(8,128)(2,1)}), bf16[6,512,256]{2,1,0:T(8,128)(2,1)}) %all-gather.2.cloned.1.call-update) | async-done | bytes 1572880 | tf_op jit(solution)/shard_map/all_gather | solution.py:69
  37.8 1.3 collective-permute-start.1
  39.1 5.2 collective-permute-start
  44.4 9.1 %slice_bitcast_fusion = (bf16[6,4,256,256]{3,2,1,0:T(8,128)(2,1)}, bf16[6,4,256,256]{3,2,1,0:T(8,128)(2,1)}, bf16[6,4,256,256]{3,2,1,0:T(8,128)(2,1)}, bf16[6,4,256,256]{3,2,1,0:T(8,128)(2,1)}) fusion(bf16[6,4,4,256,256]{4,3,2,1,0:T(8,128)(2,1)} %param.6), kind=kLoop, calls=%fused_computation.121 | loop fusion | bytes 25165824 | tf_op jit(solution)/shard_map/mul | solution.py:58
  53.9 11.7 %bitcast_multiply_fusion = (bf16[6,4,768,256]{3,2,1,0:T(8,128)(2,1)}, bf16[6,4,768,256]{3,2,1,0:T(8,128)(2,1)}) fusion(bf16[6,4,256,256]{3,2,1,0:T(8,128)(2,1)} %get-tuple-element.8, bf16[6,4,768]{2,1,0:T(4,128)(2,1)S(1)} %bitcast.75, bf16[6,4,256,256]{3,2,1,0:T(8,128)(2,1)} %get-tuple-element.11, bf16[6,4,768]{2,1,0:T(4,128)(2,1)S(1)} %bitcast.73), kind=kLoop, calls=%fused_computation.80 | loop fusion | flops 9437184 | bytes 25239552 | tf_op jit(solution)/shard_map/mul | solution.py:58
  65.8 7.7 %bitcast_multiply_fusion.2 = (bf16[6,4,768,256]{3,2,1,0:T(8,128)(2,1)}, bf16[6,4,768,256]{3,2,1,0:T(8,128)(2,1)}) fusion(bf16[6,4,256,256]{3,2,1,0:T(8,128)(2,1)S(1)} %copy-done, bf16[6,4,768]{2,1,0:T(4,128)(2,1)S(1)} %bitcast.74, bf16[6,4,256,256]{3,2,1,0:T(8,128)(2,1)S(1)} %copy-done.1, bf16[6,4,768]{2,1,0:T(4,128)(2,1)S(1)} %bitcast.72), kind=kLoop, calls=%fused_computation.82 | loop fusion | flops 9437184 | bytes 25239552 | tf_op jit(solution)/shard_map/mul | solution.py:58
  73.9 1.7 slice_add_fusion.24
  77.7 12.3 %convolution_reduce_fusion.1 = f32[6,256,512]{2,1,0:T(8,128)} fusion(bf16[6,4,768,256]{3,2,1,0:T(8,128)(2,1)} %get-tuple-element.42, bf16[6,512,256]{2,1,0:T(8,128)(2,1)} %collective-permute-done.1, bf16[6,512,256]{2,1,0:T(8,128)(2,1)} %all-gather.2.cloned.1.call-done, bf16[6,512,256]{2,1,0:T(8,128)(2,1)} %collective-permute-done), kind=kOutput, calls=%fused_computation.126 | convolution fusion | flops 4848353280 | bytes 17301504 | tf_op jit(solution)/shard_map/vrk,vskt->vsrt/dot_general | solution.py:61
  90.1 5.5 bitcast_multiply_fusion.5
  95.6 8.9 %pad_maximum_fusion.2 = f32[18,512,256]{1,2,0:T(8,128)} fusion(f32[6,512,256]{1,2,0:T(8,128)} %get-tuple-element.23, f32[6,512,256]{1,2,0:T(8,128)} %get-tuple-element.22, f32[6,512,256]{1,2,0:T(8,128)} %bitcast.69), kind=kLoop, calls=%fused_computation.78 | loop fusion | flops 4718592 | bytes 18874368 | tf_op jit(solution)/shard_map/concatenate | solution.py:82
  104.5 46.5 %fusion.20 = bf16[18,512,256]{1,2,0:T(8,128)(2,1)} fusion(f32[18,512,256]{1,2,0:T(8,128)} %pad_maximum_fusion.2), kind=kLoop, calls=%fused_computation.44 | loop fusion | flops 16515072 | bytes 14155776 | tf_op jit(solution)/shard_map/convert_element_type | solution.py:85
  151.0 1.0 fusion.60
  152.1 1.3 collective-permute-start.9
  153.4 4.0 collective-permute-start.8
  157.4 12.4 %convolution_reduce_fusion = f32[6,256,512]{2,1,0:T(8,128)} fusion(bf16[6,4,768,256]{3,2,1,0:T(8,128)(2,1)} %get-tuple-element.41, bf16[6,512,256]{2,1,0:T(8,128)(2,1)} %collective-permute-done.1, bf16[6,512,256]{2,1,0:T(8,128)(2,1)S(1)} %copy-done.4, bf16[6,512,256]{2,1,0:T(8,128)(2,1)} %collective-permute-done), kind=kOutput, calls=%fused_computation.125 | convolution fusion | flops 4848353280 | bytes 17301504 | tf_op jit(solution)/shard_map/vrk,vskt->vsrt/dot_general | solution.py:61
  169.8 5.5 bitcast_multiply_fusion.4
  175.3 9.0 %pad_maximum_fusion.3 = f32[18,512,256]{1,2,0:T(8,128)} fusion(f32[6,512,256]{1,2,0:T(8,128)} %get-tuple-element.21, f32[6,512,256]{1,2,0:T(8,128)} %get-tuple-element.20, f32[6,512,256]{1,2,0:T(8,128)} %bitcast.70), kind=kLoop, calls=%fused_computation.79 | loop fusion | flops 4718592 | bytes 18874368 | tf_op jit(solution)/shard_map/concatenate | solution.py:82
  184.3 34.7 %fusion.27 = bf16[18,512,256]{1,2,0:T(8,128)(2,1)} fusion(f32[18,512,256]{1,2,0:T(8,128)} %pad_maximum_fusion.3), kind=kLoop, calls=%fused_computation.51 | loop fusion | flops 16515072 | bytes 14155776 | tf_op jit(solution)/shard_map/convert_element_type | solution.py:85
  220.1 1.3 collective-permute-start.11
  221.4 4.0 collective-permute-start.10
  225.4 12.7 %convolution_reduce_fusion.3 = f32[6,256,512]{2,1,0:T(8,128)} fusion(bf16[6,4,768,256]{3,2,1,0:T(8,128)(2,1)} %get-tuple-element.44, bf16[6,512,256]{2,1,0:T(8,128)(2,1)} %collective-permute-done.1, bf16[6,512,256]{2,1,0:T(8,128)(2,1)S(1)} %copy-done.4, bf16[6,512,256]{2,1,0:T(8,128)(2,1)} %collective-permute-done), kind=kOutput, calls=%fused_computation.128 | convolution fusion | flops 4848353280 | bytes 17301504 | tf_op jit(solution)/shard_map/vrk,vskt->vsrt/dot_general | solution.py:61
  238.1 5.4 bitcast_multiply_fusion.7
  243.5 8.9 %pad_maximum_fusion = f32[18,512,256]{1,2,0:T(8,128)} fusion(f32[6,512,256]{1,2,0:T(8,128)} %get-tuple-element.27, f32[6,512,256]{1,2,0:T(8,128)} %get-tuple-element.26, f32[6,512,256]{1,2,0:T(8,128)} %bitcast.71), kind=kLoop, calls=%fused_computation.76 | loop fusion | flops 4718592 | bytes 18874368 | tf_op jit(solution)/shard_map/concatenate | solution.py:82
  252.5 33.5 %fusion.6 = bf16[18,512,256]{1,2,0:T(8,128)(2,1)} fusion(f32[18,512,256]{1,2,0:T(8,128)} %pad_maximum_fusion), kind=kLoop, calls=%fused_computation.30 | loop fusion | flops 16515072 | bytes 14155776 | tf_op jit(solution)/shard_map/convert_element_type | solution.py:85
  287.7 1.3 collective-permute-start.3
  289.0 12.4 %convolution_reduce_fusion.2 = f32[6,256,512]{2,1,0:T(8,128)} fusion(bf16[6,4,768,256]{3,2,1,0:T(8,128)(2,1)} %get-tuple-element.43, bf16[6,512,256]{2,1,0:T(8,128)(2,1)} %collective-permute-done.1, bf16[6,512,256]{2,1,0:T(8,128)(2,1)S(1)} %copy-done.4, bf16[6,512,256]{2,1,0:T(8,128)(2,1)} %collective-permute-done), kind=kOutput, calls=%fused_computation.127 | convolution fusion | flops 4848353280 | bytes 17301504 | tf_op jit(solution)/shard_map/vrk,vskt->vsrt/dot_general | solution.py:61
  301.4 5.4 bitcast_multiply_fusion.6
  306.8 8.9 %pad_maximum_fusion.1 = f32[18,512,256]{1,2,0:T(8,128)} fusion(f32[6,512,256]{1,2,0:T(8,128)} %get-tuple-element.25, f32[6,512,256]{1,2,0:T(8,128)} %get-tuple-element.24, f32[6,512,256]{1,2,0:T(8,128)} %bitcast.68), kind=kLoop, calls=%fused_computation.77 | loop fusion | flops 4718592 | bytes 18874368 | tf_op jit(solution)/shard_map/concatenate | solution.py:82
  315.7 33.7 %fusion.13 = bf16[18,512,256]{1,2,0:T(8,128)(2,1)} fusion(f32[18,512,256]{1,2,0:T(8,128)} %pad_maximum_fusion.1), kind=kLoop, calls=%fused_computation.37 | loop fusion | flops 16515072 | bytes 14155776 | tf_op jit(solution)/shard_map/convert_element_type | solution.py:85
  351.8 4.8 collective-permute-start.2
  356.6 1.3 collective-permute-start.7
  358.0 7.6 %maximum_convert_fusion.2 = f32[18,512,262]{1,2,0:T(8,128)} fusion(bf16[18,512,3]{1,2,0:T(4,128)(2,1)S(1)} %copy.69, bf16[18,512,256]{1,2,0:T(8,128)(2,1)} %fusion.20, bf16[18,512,3]{1,2,0:T(4,128)(2,1)S(1)} %copy.68), kind=kLoop, calls=%fused_computation.86 | loop fusion | flops 14487552 | bytes 14487552 | tf_op jit(solution)/shard_map/convert_element_type | solution.py:85
  365.6 31.4 %slice_add_fusion.6 = f32[18,512,256]{1,2,0:T(8,128)} fusion(f32[18,512,262]{1,2,0:T(8,128)} %maximum_convert_fusion.2), kind=kLoop, calls=%fused_computation.58 | loop fusion | flops 14155776 | bytes 75497472 | tf_op jit(solution)/shard_map/add | solution.py:42
  397.0 6.2 %collective-permute-start.6 = (bf16[18,512,3]{1,0,2:T(8,128)(2,1)}, bf16[18,512,3]{1,0,2:T(8,128)(2,1)S(1)}, u32[]{:S(2)}, u32[]{:S(2)}) collective-permute-start(bf16[18,512,3]{1,0,2:T(8,128)(2,1)} %copy.60), channel_id=1, source_target_pairs={{0,8},{8,16},{16,24},{24,32},{32,40},{40,48},{48,56},{56,64},{64,7... | collective-permute-start | bytes 165896 | tf_op jit(solution)/shard_map/ppermute | solution.py:20
  403.4 5.3 maximum_convert_fusion.3
  408.6 31.6 %slice_add_fusion = f32[18,512,256]{1,2,0:T(8,128)} fusion(f32[18,512,262]{1,2,0:T(8,128)} %maximum_convert_fusion.3), kind=kLoop, calls=%fused_computation.52 | loop fusion | flops 14155776 | bytes 75497472 | tf_op jit(solution)/shard_map/add | solution.py:42
  442.1 7.6 %maximum_convert_fusion = f32[18,512,262]{1,2,0:T(8,128)} fusion(bf16[18,512,3]{1,2,0:T(4,128)(2,1)S(1)} %copy.55, bf16[18,512,256]{1,2,0:T(8,128)(2,1)} %fusion.6, bf16[18,512,3]{1,2,0:T(4,128)(2,1)S(1)} %copy.54), kind=kLoop, calls=%fused_computation.84 | loop fusion | flops 14487552 | bytes 14487552 | tf_op jit(solution)/shard_map/convert_element_type | solution.py:85
  449.7 31.4 %slice_add_fusion.18 = f32[18,512,256]{1,2,0:T(8,128)} fusion(f32[18,512,262]{1,2,0:T(8,128)} %maximum_convert_fusion), kind=kLoop, calls=%fused_computation.70 | loop fusion | flops 14155776 | bytes 75497472 | tf_op jit(solution)/shard_map/add | solution.py:42
  482.2 5.3 maximum_convert_fusion.1
  487.4 31.5 %slice_add_fusion.12 = f32[18,512,256]{1,2,0:T(8,128)} fusion(f32[18,512,262]{1,2,0:T(8,128)} %maximum_convert_fusion.1), kind=kLoop, calls=%fused_computation.64 | loop fusion | flops 14155776 | bytes 75497472 | tf_op jit(solution)/shard_map/add | solution.py:42
  518.9 14.4 %fusion.51 = (f32[512,256]{0,1:T(8,128)S(1)}, f32[512,256]{0,1:T(8,128)S(1)}, f32[512,256]{0,1:T(8,128)S(1)}, f32[512,256]{0,1:T(8,128)S(1)}) fusion(f32[18,512,256]{1,2,0:T(8,128)} %slice_add_fusion.18, f32[512,256]{0,1:T(8,128)S(1)} %copy-done.3, f32[512,256]{0,1:T(8,128)S(1)} %copy-done.2, f32[18,512,256]{1,2,0:T(8,128)} %slice_add_fusion.12, ...), kind=kLoop, calls=%fused_computation.119 | loop fusion | flops 34078720 | bytes 40894464 | tf_op jit(solution)/shard_map/reduce_sum | solution.py:94
  533.3 1.3 minimum_minimum_fusion
  534.7 1.4 pad_maximum_fusion.4
  536.0 1.8 copy.76
  537.9 65.6 %all-reduce.7.cloned.1.call-done = f32[512,256]{0,1:T(8,128)} async-done(((f32[512,256]{0,1:T(8,128)}), f32[512,256]{0,1:T(8,128)}) %all-reduce.7.cloned.1.call-update) | async-done | bytes 524304 | tf_op jit(solution)/shard_map/pmin | solution.py:99
  (80 shorter events, 15.7 us)
Async XLA Ops:
  7.2 30.7 %all-gather.2.cloned.1.call-start = ((), (), s32[]{:S(2)}) async-start(), calls=%async_computation | async-start | bytes 1769472 | tf_op jit(solution)/shard_map/all_gather | solution.py:69
  7.9 595.5 %all-reduce.7.cloned.1.call-start = ((), (), s32[]{:S(2)}) async-start(), calls=%async_computation.1 | async-start | bytes 1048576 | tf_op jit(solution)/shard_map/pmin | solution.py:99
  23.6 49.9 %collective-permute-start.4 = (bf16[2,512,3]{2,1,0:T(8,128)(2,1)S(1)}, bf16[2,512,3]{2,1,0:T(8,128)(2,1)S(1)}, u32[]{:S(2)}, u32[]{:S(2)}) collective-permute-start(bf16[2,512,3]{2,1,0:T(8,128)(2,1)S(1)} %get-tuple-element.35), channel_id=1, source_target_pairs={{0,8},{8,16},{16,24},{24,32},{32,40},{40,48},{48,56},{56,64},{64,7... | collective-permute-start | bytes 18440 | tf_op jit(solution)/shard_map/ppermute | solution.py:20
  27.2 46.3 %collective-permute-start.5 = (bf16[2,512,3]{2,1,0:T(8,128)(2,1)S(1)}, bf16[2,512,3]{2,1,0:T(8,128)(2,1)S(1)}, u32[]{:S(2)}, u32[]{:S(2)}) collective-permute-start(bf16[2,512,3]{2,1,0:T(8,128)(2,1)S(1)} %get-tuple-element.36), channel_id=1, source_target_pairs={{8,0},{16,8},{24,16},{32,24},{40,32},{48,40},{56,48},{64,56},{72,6... | collective-permute-start | bytes 18440 | tf_op jit(solution)/shard_map/ppermute | solution.py:22
  37.8 39.9 %collective-permute-start.1 = (bf16[6,512,256]{2,1,0:T(8,128)(2,1)}, bf16[6,512,256]{2,1,0:T(8,128)(2,1)}, u32[]{:S(2)}, u32[]{:S(2)}) collective-permute-start(bf16[6,512,256]{2,1,0:T(8,128)(2,1)} %all-gather.2.cloned.1.call-done), channel_id=1, source_target_pairs={{8,0},{16,8},{24,16},{32,24},{40,32},{48,40},{56,48},{64,56},{72,6... | collective-permute-start | bytes 4718600 | tf_op jit(solution)/shard_map/ppermute | solution.py:22
  39.1 38.6 %collective-permute-start = (bf16[6,512,256]{2,1,0:T(8,128)(2,1)}, bf16[6,512,256]{2,1,0:T(8,128)(2,1)}, u32[]{:S(2)}, u32[]{:S(2)}) collective-permute-start(bf16[6,512,256]{2,1,0:T(8,128)(2,1)} %all-gather.2.cloned.1.call-done), channel_id=1, source_target_pairs={{0,8},{8,16},{16,24},{24,32},{32,40},{40,48},{48,56},{56,64},{64,7... | collective-permute-start | bytes 4718600 | tf_op jit(solution)/shard_map/ppermute | solution.py:20
  53.8 11.9 %copy-start = (bf16[6,4,256,256]{3,2,1,0:T(8,128)(2,1)S(1)}, bf16[6,4,256,256]{3,2,1,0:T(8,128)(2,1)}, u32[]{:S(2)}) copy-start(bf16[6,4,256,256]{3,2,1,0:T(8,128)(2,1)} %get-tuple-element.9) | copy-start | bytes 9437188
  53.9 11.9 %copy-start.1 = (bf16[6,4,256,256]{3,2,1,0:T(8,128)(2,1)S(1)}, bf16[6,4,256,256]{3,2,1,0:T(8,128)(2,1)}, u32[]{:S(2)}) copy-start(bf16[6,4,256,256]{3,2,1,0:T(8,128)(2,1)} %get-tuple-element.10) | copy-start | bytes 9437188
  104.5 52.9 %copy-start.4 = (bf16[6,512,256]{2,1,0:T(8,128)(2,1)S(1)}, bf16[6,512,256]{2,1,0:T(8,128)(2,1)}, u32[]{:S(2)}) copy-start(bf16[6,512,256]{2,1,0:T(8,128)(2,1)} %all-gather.2.cloned.1.call-done) | copy-start | bytes 4718596
  152.1 199.7 %collective-permute-start.9 = (bf16[18,512,3]{1,0,2:T(8,128)(2,1)S(1)}, bf16[18,512,3]{1,0,2:T(8,128)(2,1)S(1)}, u32[]{:S(2)}, u32[]{:S(2)}) collective-permute-start(bf16[18,512,3]{1,0,2:T(8,128)(2,1)S(1)} %copy.67), channel_id=1, source_target_pairs={{8,0},{16,8},{24,16},{32,24},{40,32},{48,40},{56,48},{64,56},{72,6... | collective-permute-start | bytes 165896 | tf_op jit(solution)/shard_map/ppermute | solution.py:22
  153.4 203.2 %collective-permute-start.8 = (bf16[18,512,3]{1,0,2:T(8,128)(2,1)S(1)}, bf16[18,512,3]{1,0,2:T(8,128)(2,1)S(1)}, u32[]{:S(2)}, u32[]{:S(2)}) collective-permute-start(bf16[18,512,3]{1,0,2:T(8,128)(2,1)S(1)} %copy.66), channel_id=1, source_target_pairs={{0,8},{8,16},{16,24},{24,32},{32,40},{40,48},{48,56},{56,64},{64,7... | collective-permute-start | bytes 165896 | tf_op jit(solution)/shard_map/ppermute | solution.py:20
  220.1 176.9 %collective-permute-start.11 = (bf16[18,512,3]{1,0,2:T(8,128)(2,1)S(1)}, bf16[18,512,3]{1,0,2:T(8,128)(2,1)S(1)}, u32[]{:S(2)}, u32[]{:S(2)}) collective-permute-start(bf16[18,512,3]{1,0,2:T(8,128)(2,1)S(1)} %copy.73), channel_id=1, source_target_pairs={{8,0},{16,8},{24,16},{32,24},{40,32},{48,40},{56,48},{64,56},{72,6... | collective-permute-start | bytes 165896 | tf_op jit(solution)/shard_map/ppermute | solution.py:22
  221.4 181.9 %collective-permute-start.10 = (bf16[18,512,3]{1,0,2:T(8,128)(2,1)S(1)}, bf16[18,512,3]{1,0,2:T(8,128)(2,1)S(1)}, u32[]{:S(2)}, u32[]{:S(2)}) collective-permute-start(bf16[18,512,3]{1,0,2:T(8,128)(2,1)S(1)} %copy.72), channel_id=1, source_target_pairs={{0,8},{8,16},{16,24},{24,32},{32,40},{40,48},{48,56},{56,64},{64,7... | collective-permute-start | bytes 165896 | tf_op jit(solution)/shard_map/ppermute | solution.py:20
  287.7 152.5 %collective-permute-start.3 = (bf16[18,512,3]{1,0,2:T(8,128)(2,1)}, bf16[18,512,3]{1,0,2:T(8,128)(2,1)}, u32[]{:S(2)}, u32[]{:S(2)}) collective-permute-start(bf16[18,512,3]{1,0,2:T(8,128)(2,1)} %copy.53), channel_id=1, source_target_pairs={{8,0},{16,8},{24,16},{32,24},{40,32},{48,40},{56,48},{64,56},{72,6... | collective-permute-start | bytes 165896 | tf_op jit(solution)/shard_map/ppermute | solution.py:22
  351.8 89.4 %collective-permute-start.2 = (bf16[18,512,3]{1,0,2:T(8,128)(2,1)S(1)}, bf16[18,512,3]{1,0,2:T(8,128)(2,1)}, u32[]{:S(2)}, u32[]{:S(2)}) collective-permute-start(bf16[18,512,3]{1,0,2:T(8,128)(2,1)S(1)} %copy.52), channel_id=1, source_target_pairs={{0,8},{8,16},{16,24},{24,32},{32,40},{40,48},{48,56},{56,64},{64,7... | collective-permute-start | bytes 165896 | tf_op jit(solution)/shard_map/ppermute | solution.py:20
  356.6 124.6 %collective-permute-start.7 = (bf16[18,512,3]{1,0,2:T(8,128)(2,1)}, bf16[18,512,3]{1,0,2:T(8,128)(2,1)}, u32[]{:S(2)}, u32[]{:S(2)}) collective-permute-start(bf16[18,512,3]{1,0,2:T(8,128)(2,1)} %copy.61), channel_id=1, source_target_pairs={{8,0},{16,8},{24,16},{32,24},{40,32},{48,40},{56,48},{64,56},{72,6... | collective-permute-start | bytes 165896 | tf_op jit(solution)/shard_map/ppermute | solution.py:22
  357.9 45.4 %slice-start = ((s8[4718592]{0:T(1024)(128)(4,1)}), s8[4194304]{0:T(1024)(128)(4,1)S(1)}, s32[]{:S(2)}) async-start(s8[4718592]{0:T(1024)(128)(4,1)} %bitcast.64), calls=%async_computation.2 | async-start | bytes 8388608
  365.6 37.8 %slice-start.1 = ((s8[4718592]{0:T(1024)(128)(4,1)}), s8[524288]{0:T(1024)(128)(4,1)S(1)}, s32[]{:S(2)}) async-start(s8[4718592]{0:T(1024)(128)(4,1)} %bitcast.64), calls=%async_computation.3 | async-start | bytes 1048576
  397.0 85.1 %collective-permute-start.6 = (bf16[18,512,3]{1,0,2:T(8,128)(2,1)}, bf16[18,512,3]{1,0,2:T(8,128)(2,1)S(1)}, u32[]{:S(2)}, u32[]{:S(2)}) collective-permute-start(bf16[18,512,3]{1,0,2:T(8,128)(2,1)} %copy.60), channel_id=1, source_target_pairs={{0,8},{8,16},{16,24},{24,32},{32,40},{40,48},{48,56},{56,64},{64,7... | collective-permute-start | bytes 165896 | tf_op jit(solution)/shard_map/ppermute | solution.py:20
  442.1 40.1 %slice-start.2 = ((s8[4718592]{0:T(1024)(128)(4,1)}), s8[4194304]{0:T(1024)(128)(4,1)S(1)}, s32[]{:S(2)}) async-start(s8[4718592]{0:T(1024)(128)(4,1)} %bitcast.66), calls=%async_computation.4 | async-start | bytes 8388608
  449.7 32.4 %slice-start.3 = ((s8[4718592]{0:T(1024)(128)(4,1)}), s8[524288]{0:T(1024)(128)(4,1)S(1)}, s32[]{:S(2)}) async-start(s8[4718592]{0:T(1024)(128)(4,1)} %bitcast.66), calls=%async_computation.5 | async-start | bytes 1048576
  487.4 31.5 %copy-start.2 = (f32[512,256]{0,1:T(8,128)S(1)}, f32[512,256]{0,1:T(8,128)}, u32[]{:S(2)}) copy-start(f32[512,256]{0,1:T(8,128)} %copy.56) | copy-start | bytes 1572868
  487.4 31.5 %copy-start.3 = (f32[512,256]{0,1:T(8,128)S(1)}, f32[512,256]{0,1:T(8,128)}, u32[]{:S(2)}) copy-start(f32[512,256]{0,1:T(8,128)} %copy.57) | copy-start | bytes 1572868
Sparse Core Ops, SparseCore 0:
  9.7 28.0 all-gather.1
  534.8 68.6 all-reduce.6
where the time goes:
time: 622 us; the launch traced here: 612 us
  other arithmetic  398 us (64%)
  waiting for transfers between devices  74.6 us (12%)
  matrix products  49.8 us (8%)
  starting transfers between devices  35.5 us (6%)
  local copies, waits for them, and re-layouts  24.8 us (4%)
  between operations  14.9 us (2%)
  blocking collectives  14.7 us (2%)
    convert_element_type x4, other arithmetic, local(): stat_rows.astype(jnp.bfloat16)  148 us
    add x5, other arithmetic, column_box(): summed = summed + extended[..., offset_col:offset_col + width_tile]  128 us
    pmin x1, waiting for transfers between devices, local(): everywhere = lax.pmin(lowest, 'plane')  65.6 us
    dot_general x4, matrix products, warp_plane(): jnp.einsum('vrk,vskt->vsrt', wide_src, placed, preferred_element_type=jnp...  49.8 us
    concatenate x4, other arithmetic, local(): jnp.concatenate([warped, warped * warped, ref_float[None] * warped], axis=0)  35.7 us
    ppermute x6, starting transfers between devices, extended_2(): lax.ppermute(tail, axis, [(i, (i + 1) % count) for i in range(ends)])  27.7 us
    convert_element_type x4, other arithmetic, local(): extended_2(stat_rows.astype(jnp.bfloat16), (('tile', 2),), HALF)  25.8 us
    mul x4, other arithmetic, local(): warped * warped  21.8 us
  transfers between devices with their start and end apart: 14, of which 2 were waited for; matrix products, arithmetic and copies ran while one was open for 56% of the time, Pallas kernels for 0%

commit v1 on v0

v1 whole, which is shorter than its diff:
```python
import functools

import jax
import jax.numpy as jnp
from jax import lax
from jax.experimental import pallas as pl
from jax.experimental.pallas import tpu as pltpu
from jax.sharding import PartitionSpec as P

MESH = pl.DeviceIdType.MESH
HALF = 3
COUNT = float((2 * HALF + 1) ** 2)
STABILIZER = 4.0
TW = 256
SUB = 8
RUN = 32
PART = SUB * RUN
F32 = jnp.float32
BF16 = jnp.bfloat16


def iota(shape, dim):
    return lax.broadcasted_iota(jnp.int32, shape, dim)


def third(x):
    return (x * 171) >> 9


def as01(mask):
    return jnp.where(mask, 1.0, 0.0).astype(BF16)


def mm(a, b):
    return jnp.dot(a, b, preferred_element_type=F32)


def split2(x):
    hi = x.astype(BF16)
    return hi, (x - hi.astype(F32)).astype(BF16)


def body(
    views,
    planes,
    tiles,
    nq,
    ref_hbm,
    src_hbm,
    warp_hbm,
    off_ref,
    vol_hbm,
    best_ref,
    *scratch,
):
    srcs = scratch[:views]
    (
        ref_all,
        warp,
        picked,
        wb,
        rb,
        sums,
        acc,
        rn,
        inv,
        slab,
        slab16,
        halo,
        band,
        perm,
        unperm,
        edge_t,
        edge_q,
        esums,
        vol,
        low,
        got1,
        red,
        got2,
        s1_send,
        s1_recv,
        own_sem,
        z_send,
        z_recv,
        f_send,
        f_recv,
        w_sem,
        h_send,
        h_recv,
        m_send,
        m_recv,
        out_sem,
    ) = scratch[views:]
    nx = nq // 2
    rows = nq * ref_hbm.shape[0]
    halves = rows // PART
    t = lax.axis_index("tile")
    q = lax.axis_index("plane")
    x = q // 2
    c = q % 2
    sib = 2 * x + 1 - c
    has_left = t > 0
    has_right = t < tiles - 1
    left = lax.rem(t + tiles - 1, tiles)
    right = lax.rem(t + 1, tiles)

    def at_x(d):
        return lax.rem(x + d + nx, nx)

    def remote(src, dst, ssem, rsem, dev):
        return pltpu.make_async_remote_copy(
            src_ref=src,
            dst_ref=dst,
            send_sem=ssem,
            recv_sem=rsem,
            device_id=dev,
            device_id_type=MESH,
        )

    def piece(k):
        return ref_hbm if k == views else src_hbm.at[k]

    def slot(k, xx, cc):
        return ref_all.at[xx, cc] if k == views else srcs[k].at[1, xx, cc]

    def column(k, cc):
        if k == views:
            return ref_all.at[:, pl.ds(cc, 1)]
        return srcs[k].at[1, :, pl.ds(cc, 1)]

    def own_copy(k):
        return pltpu.make_async_copy(piece(k), slot(k, x, c), own_sem.at[k])

    def x_send(k, d):
        return remote(
            piece(k), slot(k, x, c), s1_send.at[k, d - 1], s1_recv.at[k, d - 1], (t, 2 * at_x(d) + c)
        )

    def x_arrival(k, d):
        return remote(
            piece(k), slot(k, at_x(-d), c), s1_send.at[k, d - 1], s1_recv.at[k, d - 1], (t, 2 * at_x(d) + c)
        )

    def z_copy(k, side):
        return remote(
            column(k, c),
            srcs[k].at[2 * side, :, pl.ds(c, 1)],
            z_send.at[k, side],
            z_recv.at[k, side],
            (right if side == 0 else left, q),
        )

    def to_sib(k, block):
        source = column(k, c) if block == 1 else srcs[k].at[block, :, pl.ds(c, 1)]
        return remote(source, source, f_send.at[k, block], f_recv.at[k, block], (t, sib))

    def from_sib(k, block):
        target = column(k, 1 - c) if block == 1 else srcs[k].at[block, :, pl.ds(1 - c, 1)]
        return remote(target, target, f_send.at[k, block], f_recv.at[k, block], (t, sib))

    def when_arrives(side, fn):
        pl.when(has_left if side == 0 else has_right)(fn)

    def when_sends(side, fn):
        pl.when(has_right if side == 0 else has_left)(fn)

    def stage1(k):
        for d in range(1, nx):
            x_send(k, d).start()
        own_copy(k).start()

    def stage2(k):
        own_copy(k).wait()
        for d in range(1, nx):
            x_arrival(k, d).wait_recv()
        if k < views:
            for side in (0, 1):
                when_sends(side, lambda side=side: z_copy(k, side).start())
        to_sib(k, 1).start()

    def stage3(k):
        for side in (0, 1):

            @functools.partial(when_arrives, side)
            def _():
                z_copy(k, side).wait_recv()
                to_sib(k, 2 * side).start()

    def finish(k):
        from_sib(k, 1).wait_recv()
        if k < views:
            for side in (0, 1):
                when_arrives(side, lambda side=side: from_sib(k, 2 * side).wait_recv())

    def drain(k):
        for d in range(1, nx):
            x_send(k, d).wait_send()
        to_sib(k, 1).wait_send()
        if k < views:
            for side in (0, 1):
                when_sends(side, lambda side=side: z_copy(k, side).wait_send())
                when_arrives(side, lambda side=side: to_sib(k, 2 * side).wait_send())

    def warp_copy(k):
        return pltpu.make_async_copy(warp_hbm.at[k], warp.at[k], w_sem.at[k])

    def halo_copy(side):
        return remote(
            slab16.at[side], halo.at[side], h_send.at[side], h_recv.at[side], (right if side == 0 else left, q)
        )

    barrier = pltpu.get_barrier_semaphore()
    partners = [(t, 2 * at_x(d) + c) for d in range(1, nx)] + [(t, sib), (left, q), (right, q)]
    for dev in partners:
        pl.semaphore_signal(barrier, inc=1, device_id=dev, device_id_type=MESH)
    pl.semaphore_wait(barrier, len(partners))

    stage1(0)
    stage1(views)
    warp_copy(0).start()
    for k in range(1, views):
        stage1(k)
    for k in range(1, views):
        warp_copy(k).start()

    ri, ci = iota((TW, TW), 0), iota((TW, TW), 1)
    band[...] = as01(jnp.abs(ri - ci) <= HALF)
    perm[...] = as01(((ri & (SUB - 1)) * RUN + (ri >> 3)) == ci)
    unperm[...] = as01(((ci & (SUB - 1)) * RUN + (ci >> 3)) == ri)
    rk, cl = iota((384, 128), 0), iota((384, 128), 1)
    kk = rk & 127
    ki, li = third(kk), third(cl)
    gap = (rk >> 7) * 3 - 3 + (kk - 3 * ki) - (cl - 3 * li)
    edge_t[...] = as01((ki == li) & (jnp.abs(gap) <= HALF))
    rq, cq = iota((128, 128), 0), iota((128, 128), 1)
    r_lane = 3 * views * planes
    edge_q[...] = as01(rq == r_lane + cq - 3 * third(cq))
    slab[...] = jnp.zeros_like(slab)
    acc[...] = jnp.zeros_like(acc)

    @pl.when(jnp.logical_not(has_left))
    def _():
        halo[0] = jnp.zeros_like(halo[0])
        for k in range(views):
            srcs[k][0] = jnp.zeros_like(srcs[k][0])

    @pl.when(jnp.logical_not(has_right))
    def _():
        halo[1] = jnp.zeros_like(halo[1])
        for k in range(views):
            srcs[k][2] = jnp.zeros_like(srcs[k][2])

    lane = iota((rows, 128), 1)

    def pack(w, i):
        first = 3 * i
        here = (lane >= first) & (lane < first + 3)
        wl, wr = w[:, :128], w[:, 128:]
        for n, (part, shift) in enumerate(((wl, 0), (wl, 125), (wr, 6), (wr, 3))):
            slab[n] = jnp.where(here, pltpu.roll(part, lax.rem(first + shift, 128), 1), slab[n])

    def permute(value):
        return jnp.concatenate(
            [mm(perm[...], value[PART * h : PART * (h + 1)]).astype(BF16) for h in range(halves)], axis=0
        )

    def put_sums(target, n, value):
        wide = value.shape[1]
        cells = value.reshape(halves, RUN, SUB, wide)
        sub = iota((HALF, SUB, wide), 1)
        target[n, :, HALF : HALF + RUN] = cells
        before = [pltpu.roll(cells[h, RUN - HALF :], 1, 1) for h in range(halves)]
        after = [pltpu.roll(cells[h, :HALF], SUB - 1, 1) for h in range(halves)]
        zero = jnp.zeros((HALF, SUB, wide), F32)
        for h in range(halves):
            target[n, h, :HALF] = jnp.where(sub == 0, before[h - 1] if h else zero, before[h])
            target[n, h, HALF + RUN :] = jnp.where(
                sub == SUB - 1, after[h + 1] if h + 1 < halves else zero, after[h]
            )

    def row_sums(source, n, h, first, size, lanes):
        v = source[n, h, pl.ds(first, size + 6), :, lanes]
        two = v[: size + 5] + v[1 : size + 6]
        four = two[:size] + two[2 : size + 2]
        return (four + two[4 : size + 4]) + v[6 : size + 6]

    stage2(0)
    stage2(views)
    if views > 1:
        stage2(1)
    finish(views)

    r = permute(ref_all[...].reshape(rows, TW))
    rb[...] = r
    rf = r.astype(F32)
    pack(rf, views * planes)
    rr_hi, rr_lo = split2(rf * rf)
    put_sums(sums, 0, mm(r, band[...]))
    put_sums(sums, 1, mm(rr_hi, band[...]) + mm(rr_lo, band[...]))
    every = pl.ds(0, TW)
    for h in range(halves):
        sr = row_sums(sums, 0, h, 0, RUN, every)
        srr = row_sums(sums, 1, h, 0, RUN, every)
        mean = sr * (1.0 / COUNT)
        rn[h] = mean
        inv[h] = lax.rsqrt(jnp.maximum(srr - sr * mean, 0.0) + STABILIZER)
    stage3(0)

    STEP = 16
    chunks = RUN // STEP

    def view_step(v, carry):
        for k in range(views):

            @pl.when(v == k)
            def _():
                if k + 2 < views:
                    stage2(k + 2)
                if k + 1 < views:
                    stage3(k + 1)
                finish(k)
                for b in range(3):
                    picked[b] = permute(srcs[k][b].reshape(rows, TW))
                warp_copy(k).wait()

        def resample(p, carry):
            w = None
            for s in range(4):
                block = off_ref[(v * planes + p) * 4 + s] + 1
                term = mm(picked[block], warp[v, p, s])
                w = term if w is None else w + term
            wb[p] = w.astype(BF16)
            pack(w, v * planes + p)
            return carry

        lax.fori_loop(0, planes, resample, 0)

        @pl.when(v == views - 1)
        def _():
            slab16[0] = slab[3].astype(BF16)
            slab16[1] = slab[0].astype(BF16)
            for side in (0, 1):
                when_sends(side, lambda side=side: halo_copy(side).start())

        def correlate(p, carry):
            w = wb[p]
            put_sums(sums, 0, mm(w, band[...]))
            put_sums(sums, 1, mm(w * w, band[...]))
            put_sums(sums, 2, mm(w * rb[...], band[...]))

            def part(n, carry):
                h = n // chunks
                first = (n % chunks) * STEP
                for lt in range(2):
                    lanes = pl.ds(128 * lt, 128)
                    sw = row_sums(sums, 0, h, first, STEP, lanes)
                    sww = row_sums(sums, 1, h, first, STEP, lanes)
                    srw = row_sums(sums, 2, h, first, STEP, lanes)
                    covar = srw - rn[h, pl.ds(first, STEP), :, lanes] * sw
                    var = jnp.maximum(sww - sw * (sw * (1.0 / COUNT)), 0.0) + STABILIZER
                    acc[p, h, pl.ds(first, STEP), :, lanes] += covar * lax.rsqrt(var)
                return carry

            lax.fori_loop(0, halves * chunks, part, 0)
            return carry

        lax.fori_loop(0, planes, correlate, 0)
        return carry

    lax.fori_loop(0, views, view_step, 0)

    for side in (0, 1):
        when_arrives(side, lambda side=side: halo_copy(side).wait_recv())

    edges = []
    for side in (0, 1):
        if side == 0:
            cells = [halo[0], slab[0].astype(BF16), slab[1].astype(BF16)]
        else:
            cells = [slab[2].astype(BF16), slab[3].astype(BF16), halo[1]]
        refs = [mm(cell, edge_q[...]).astype(BF16) for cell in cells]
        w, rw = jnp.concatenate(cells, axis=1), jnp.concatenate(refs, axis=1)
        wf, rf = w.astype(F32), rw.astype(F32)

        def summed(value):
            hi, lo = split2(value)
            return mm(hi, edge_t[...]) + mm(lo, edge_t[...])

        put_sums(esums, 0, mm(w, edge_t[...]))
        put_sums(esums, 1, summed(wf * wf))
        put_sums(esums, 2, summed(rf * wf))
        put_sums(esums, 3, mm(rw, edge_t[...]))
        put_sums(esums, 4, summed(rf * rf))
        out = []
        for h in range(halves):
            sw, sww, srw, sr, srr = [row_sums(esums, n, h, 0, RUN, pl.ds(0, 128)) for n in range(5)]
            covar = srw - sr * (sw * (1.0 / COUNT))
            var = jnp.maximum(sww - sw * (sw * (1.0 / COUNT)), 0.0) + STABILIZER
            var_r = jnp.maximum(srr - sr * (sr * (1.0 / COUNT)), 0.0) + STABILIZER
            ncc = covar * (lax.rsqrt(var) * lax.rsqrt(var_r))
            total = ncc
            for v in range(1, views):
                total = total + pltpu.roll(ncc, 128 - 3 * planes * v, 2)
            out.append(total)
        edges.append(out)

    lane3 = iota((RUN, SUB, 128), 2)

    def vol_copy(p):
        return pltpu.make_async_copy(vol.at[p], vol_hbm.at[p], out_sem.at[p])

    for p in range(planes):
        for h in range(halves):
            total = acc[p, h] * inv[h]
            lo_part, hi_part = total[:, :, :128], total[:, :, 128:]
            l_edge = pltpu.roll(edges[0][h], (128 - 3 * p) % 128, 2)
            r_edge = pltpu.roll(edges[1][h], 125 - 3 * p, 2)
            total = jnp.concatenate(
                [jnp.where(lane3 < 3, l_edge, lo_part), jnp.where(lane3 >= 125, r_edge, hi_part)], axis=2
            )
            hi, lo = split2((total * (1.0 / views)).reshape(PART, TW))
            cost = 1.0 - (mm(unperm[...], hi) + mm(unperm[...], lo))
            vol[p, PART * h : PART * (h + 1)] = cost
            per = PART * nx // rows
            cost4 = cost.reshape(per, 2, rows // nq, TW)
            spot = slice(per * h, per * (h + 1))
            low[spot] = cost4 if p == 0 else jnp.minimum(low[spot], cost4)
        vol_copy(p).start()

    swap = remote(low.at[:, pl.ds(1 - c, 1)], got1, m_send.at[0], m_recv.at[0], (t, sib))
    swap.start()
    swap.wait_recv()
    red[...] = jnp.minimum(low[:, pl.ds(c, 1)], got1[...])

    def min_copy(d):
        return remote(
            red.at[at_x(d)], got2.at[d - 1], m_send.at[d], m_recv.at[d], (t, 2 * at_x(d) + c)
        )

    for d in range(1, nx):
        min_copy(d).start()
    best = red[x, 0]
    for d in range(1, nx):
        min_copy(d).wait_recv()
        best = jnp.minimum(best, got2[d - 1, 0])
    best_ref[...] = best

    for k in range(views + 1):
        drain(k)
    for side in (0, 1):
        when_sends(side, lambda side=side: halo_copy(side).wait_send())
    swap.wait_send()
    for d in range(1, nx):
        min_copy(d).wait_send()
    for p in range(planes):
        vol_copy(p).wait()


def solution(mesh):
    tiles, nq = mesh.shape["tile"], mesh.shape["plane"]
    nx = nq // 2

    def local(reference_image, source_images, warps, offsets):
        views, planes = warps.shape[0], warps.shape[1]
        part = reference_image.shape[0]
        rows = nq * part
        halves = rows // PART
        vmem = pltpu.VMEM
        dma = pltpu.SemaphoreType.DMA
        scratch = [vmem((3, nx, 2, part, TW), BF16) for _ in range(views)] + [
            vmem((nx, 2, part, TW), BF16),
            vmem((views, planes, 4, TW, TW), BF16),
            vmem((3, rows, TW), BF16),
            vmem((planes, rows, TW), BF16),
            vmem((rows, TW), BF16),
            vmem((3, halves, RUN + 2 * HALF, SUB, TW), F32),
            vmem((planes, halves, RUN, SUB, TW), F32),
            vmem((halves, RUN, SUB, TW), F32),
            vmem((halves, RUN, SUB, TW), F32),
            vmem((4, rows, 128), F32),
            vmem((2, rows, 128), BF16),
            vmem((2, rows, 128), BF16),
            vmem((TW, TW), BF16),
            vmem((TW, TW), BF16),
            vmem((TW, TW), BF16),
            vmem((384, 128), BF16),
            vmem((128, 128), BF16),
            vmem((5, halves, RUN + 2 * HALF, SUB, 128), F32),
            vmem((planes, rows, TW), F32),
            vmem((nx, 2, part, TW), F32),
            vmem((nx, 1, part, TW), F32),
            vmem((nx, 1, part, TW), F32),
            vmem((nx - 1, 1, part, TW), F32),
            dma((views + 1, nx - 1)),
            dma((views + 1, nx - 1)),
            dma((views + 1,)),
            dma((views, 2)),
            dma((views, 2)),
            dma((views + 1, 3)),
            dma((views + 1, 3)),
            dma((views,)),
            dma((2,)),
            dma((2,)),
            dma((nx,)),
            dma((nx,)),
            dma((planes,)),
        ]
        anywhere = pl.BlockSpec(memory_space=pl.ANY)
        return pl.pallas_call(
            functools.partial(body, views, planes, tiles, nq),
            out_shape=(
                jax.ShapeDtypeStruct((planes, rows, TW), F32),
                jax.ShapeDtypeStruct((part, TW), F32),
            ),
            in_specs=[anywhere, anywhere, anywhere, pl.BlockSpec(memory_space=pltpu.SMEM)],
            out_specs=(anywhere, pl.BlockSpec(memory_space=pltpu.VMEM)),
            scratch_shapes=scratch,
            compiler_params=pltpu.CompilerParams(
                collective_id=0, has_side_effects=True, vmem_limit_bytes=58 * 1024 * 1024
            ),
        )(reference_image, source_images, warps, offsets.reshape(-1))

    return jax.shard_map(
        local,
        mesh=mesh,
        in_specs=(
            P("plane", "tile"),
            P(None, "plane", "tile"),
            P(None, "plane", None, None, "tile"),
            P(None, "plane", None, "tile"),
        ),
        out_specs=(P("plane", None, "tile"), P("plane", "tile")),
        check_vma=False,
    )
```

time: 622 us -> 78.2 us (0.13); the launches traced: 612 us -> 78 us
  other arithmetic: 398 us -> 0 us
  waiting for transfers between devices: 74.6 us -> 0 us
  Pallas kernels: 0 us -> 72.3 us
  matrix products: 49.8 us -> 0 us
  starting transfers between devices: 35.5 us -> 0 us
  local copies, waits for them, and re-layouts: 24.8 us -> 5.13 us
  blocking collectives: 14.7 us -> 0 us
  between operations: 14.9 us -> 0.65 us
    convert_element_type x14 -> x0, other arithmetic: 175 us -> none  [the longest x4 148 us: local(): stat_rows.astype(jnp.bfloat16)]
    add x6 -> x0, other arithmetic: 128 us -> none  [the longest x5 128 us: column_box(): summed = summed + extended[..., offset_col:offset_col + width_tile]]
    pallas_call x0 -> x1, Pallas kernels: none -> 72.3 us  [local(): pl.pallas_call(functools.partial(body, views, planes, tiles, nq), out_sha...]
    pmin x1 -> x0, waiting for transfers between devices: 65.6 us -> none  [local(): everywhere = lax.pmin(lowest, 'plane')]
    dot_general x4 -> x0, matrix products: 49.8 us -> none  [warp_plane(): jnp.einsum('vrk,vskt->vsrt', wide_src, placed, preferred_element_type=jnp...]
    mul x7 -> x0, other arithmetic: 41.4 us -> none  [the longest x4 21.8 us: local(): warped * warped]
    concatenate x4 -> x0, other arithmetic: 35.7 us -> none  [local(): jnp.concatenate([warped, warped * warped, ref_float[None] * warped], axis=0)]
    ppermute x12 -> x0, starting transfers between devices: 35.4 us -> none  [the longest x6 27.7 us: extended_2(): lax.ppermute(tail, axis, [(i, (i + 1) % count) for i in range(ends)])]
  transfers between devices with their start and end apart: 14 -> 0, of which waited for: 2 -> 0; matrix products, arithmetic and copies ran while one was open for 56% -> 0% of each run, Pallas kernels for 0% -> 0%
where the time goes in v1:
time: 78.2 us; the launch traced here: 78 us
  Pallas kernels  72.3 us (92%)
  local copies, waits for them, and re-layouts  5.13 us (7%)
    pallas_call x1, Pallas kernels, local(): pl.pallas_call(functools.partial(body, views, planes, tiles, nq), out_sha...  72.3 us
    unnamed x5, local copies, waits for them, and re-layouts  4.51 us

profile of v1, /device:TPU:1, one launch (start us, length us, event | category | flops | bytes accessed | tf_op | source)
XLA Modules:
  0.0 78.0 jit_solution(797378315073251435)
XLA Ops:
  0.6 0.8 %copy.7 = s32[6,4,4,1]{2,1,0,3:T(4,128)S(1)} copy(s32[6,4,4,1]{0,3,2,1:T(1,128)} %param.7) | data formatting | bytes 768 | tf_op args[3]
  1.4 0.6 reshape.7.off_ref
  2.0 72.3 %shard_map.59 = (f32[4,512,256]{2,1,0:T(8,128)}, f32[64,256]{1,0:T(8,128)}) custom-call(bf16[64,256]{1,0:T(8,128)(2,1)} %ref_hbm.1, bf16[6,64,256]{2,1,0:T(8,128)(2,1)} %src_hbm.1, bf16[6,4,4,256,256]{4,3,2,1,0:T(8,128)(2,1)} %warp_hbm.1, s32[96]{0:T(128)} %reshape.7.off_ref), custom_call_target="tpu_custom_call" | custom-call | tf_op jit(solution)/shard_map/pallas_call | solution.py:510
  74.3 0.0 copy-start
  74.3 3.1 %copy.10 = f32[4,512,256]{2,1,0:T(8,128)} copy(f32[4,512,256]{2,1,0:T(8,128)} %get-tuple-element.4) | data formatting | bytes 4194304
  77.4 0.0 copy-done
  77.4 0.6 copy.11
Async XLA Ops:
  74.3 3.1 %copy-start = (f32[64,256]{1,0:T(8,128)S(1)}, f32[64,256]{1,0:T(8,128)}, u32[]{:S(2)}) copy-start(f32[64,256]{1,0:T(8,128)} %get-tuple-element.5) | copy-start | bytes 196612

commit v2 on v1

v2 whole, which is shorter than its diff:
```python
import functools

import jax
import jax.numpy as jnp
from jax import lax
from jax.experimental import pallas as pl
from jax.experimental.pallas import tpu as pltpu
from jax.sharding import PartitionSpec as P

MESH = pl.DeviceIdType.MESH
HALF = 3
COUNT = float((2 * HALF + 1) ** 2)
STABILIZER = 4.0
TW = 256
SUB = 8
RUN = 32
PART = SUB * RUN
EDGE_SLOTS = 8
F32 = jnp.float32
BF16 = jnp.bfloat16


def iota(shape, dim):
    return lax.broadcasted_iota(jnp.int32, shape, dim)


def third(x):
    return (x * 171) >> 9


def as01(mask):
    return jnp.where(mask, 1.0, 0.0).astype(BF16)


def mm(a, b):
    return jnp.dot(a, b, preferred_element_type=F32)


def split2(x):
    hi = x.astype(BF16)
    return hi, (x - hi.astype(F32)).astype(BF16)


def body(
    views,
    planes,
    tiles,
    nq,
    ref_hbm,
    src_hbm,
    warp_hbm,
    off_ref,
    vol,
    best_ref,
    srcs,
    ref_all,
    warp,
    picked,
    wb,
    rb,
    sums_even,
    sums_odd,
    acc,
    rn,
    inv,
    slab,
    cells16,
    halo,
    band,
    perm,
    unperm,
    select,
    edge_t,
    edge_q,
    esums,
    low,
    got1,
    red,
    got2,
    s1_send,
    s1_recv,
    own_sem,
    z_send,
    z_recv,
    f_send,
    f_recv,
    w_sem,
    h_send,
    h_recv,
    p_send,
    p_recv,
    m_send,
    m_recv,
):
    nx = nq // 2
    rows = nq * ref_hbm.shape[0]
    halves = rows // PART
    per = nx // halves
    t = lax.axis_index("tile")
    q = lax.axis_index("plane")
    x = q // 2
    c = q % 2
    sib = 2 * x + 1 - c
    has_left = t > 0
    has_right = t < tiles - 1
    left = lax.rem(t + tiles - 1, tiles)
    right = lax.rem(t + 1, tiles)

    def at_x(d):
        return lax.rem(x + d + nx, nx)

    def remote(src, dst, ssem, rsem, dev):
        return pltpu.make_async_remote_copy(
            src_ref=src,
            dst_ref=dst,
            send_sem=ssem,
            recv_sem=rsem,
            device_id=dev,
            device_id_type=MESH,
        )

    REF = "ref"

    def sem_at(k):
        return views if k is REF else k

    def piece(k):
        return ref_hbm if k is REF else src_hbm.at[k]

    def slot(k, xx, cc):
        return ref_all.at[xx, cc] if k is REF else srcs.at[k, 1, xx, cc]

    def column(k, block, cc):
        if k is REF:
            return ref_all.at[:, pl.ds(cc, 1)]
        return srcs.at[k, block, :, pl.ds(cc, 1)]

    def own_copy(k):
        return pltpu.make_async_copy(piece(k), slot(k, x, c), own_sem.at[sem_at(k)])

    def x_copy(k, d, where):
        n = sem_at(k)
        return remote(
            piece(k), slot(k, where, c), s1_send.at[n, d - 1], s1_recv.at[n, d - 1], (t, 2 * at_x(d) + c)
        )

    def x_send(k, d):
        return x_copy(k, d, x)

    def x_arrival(k, d):
        return x_copy(k, d, at_x(-d))

    def z_copy(k, side):
        return remote(
            column(k, 1, c),
            column(k, 2 * side, c),
            z_send.at[k, side],
            z_recv.at[k, side],
            (right if side == 0 else left, q),
        )

    def sib_copy(k, block, cc):
        n = sem_at(k)
        place = column(k, block, cc)
        return remote(place, place, f_send.at[n, block], f_recv.at[n, block], (t, sib))

    def when_arrives(side, fn):
        pl.when(has_left if side == 0 else has_right)(fn)

    def when_sends(side, fn):
        pl.when(has_right if side == 0 else has_left)(fn)

    def stage1(k):
        for d in range(1, nx):
            x_send(k, d).start()

    def stage2(k):
        own_copy(k).wait()
        for d in range(1, nx):
            x_arrival(k, d).wait_recv()
        if k is not REF:
            for side in (0, 1):
                when_sends(side, lambda side=side: z_copy(k, side).start())
        sib_copy(k, 1, c).start()

    def stage3(k):
        for side in (0, 1):

            @functools.partial(when_arrives, side)
            def _():
                z_copy(k, side).wait_recv()
                sib_copy(k, 2 * side, c).start()

    def finish(k):
        sib_copy(k, 1, 1 - c).wait_recv()
        if k is not REF:
            for side in (0, 1):
                when_arrives(side, lambda side=side: sib_copy(k, 2 * side, 1 - c).wait_recv())

    def drain(k):
        for d in range(1, nx):
            x_send(k, d).wait_send()
        sib_copy(k, 1, c).wait_send()
        if k is not REF:
            for side in (0, 1):
                when_sends(side, lambda side=side: z_copy(k, side).wait_send())
                when_arrives(side, lambda side=side: sib_copy(k, 2 * side, c).wait_send())

    def warp_copy(k):
        return pltpu.make_async_copy(warp_hbm.at[k], warp.at[k], w_sem.at[k])

    def halo_copy(side):
        return remote(
            cells16.at[3 if side == 0 else 0],
            halo.at[side],
            h_send.at[side],
            h_recv.at[side],
            (right if side == 0 else left, q),
        )

    barrier = pltpu.get_barrier_semaphore()
    partners = [(t, 2 * at_x(d) + c) for d in range(1, nx)] + [(t, sib), (left, q), (right, q)]
    for dev in partners:
        pl.semaphore_signal(barrier, inc=1, device_id=dev, device_id_type=MESH)
    for k in [0, REF, *range(1, views)]:
        own_copy(k).start()
    for k in range(views):
        warp_copy(k).start()

    ri, ci = iota((TW, TW), 0), iota((TW, TW), 1)
    band[...] = as01(jnp.abs(ri - ci) <= HALF)
    perm[...] = as01(((ri & (SUB - 1)) * RUN + (ri >> 3)) == ci)
    unperm[...] = as01(((ci & (SUB - 1)) * RUN + (ci >> 3)) == ri)
    rk, cl = iota((384, 128), 0), iota((384, 128), 1)
    kk = rk & 127
    ki, li = third(kk), third(cl)
    gap = (rk >> 7) * 3 - 3 + (kk - 3 * ki) - (cl - 3 * li)
    edge_t[...] = as01((ki == li) & (jnp.abs(gap) <= HALF))
    rq, cq = iota((128, 128), 0), iota((128, 128), 1)
    r_lane = 3 * views * planes
    edge_q[...] = as01(rq == r_lane + cq - 3 * third(cq))
    slabs = slab.shape[0]
    rs, cs = iota((128 * slabs, 512), 0), iota((128 * slabs, 512), 1)
    cl = cs & 127
    ci3 = third(cl)
    spot = jnp.where(cl >= r_lane, EDGE_SLOTS * 12, (ci3 >> 3) * 128 + (ci3 & 7) * 12)
    wanted = spot + ((cs >> 7) ^ 2) * 3 + cl - 3 * ci3
    select[...] = as01((rs == wanted) & (cl < r_lane + 3))
    slab[...] = jnp.zeros_like(slab)
    acc[...] = jnp.zeros_like(acc)
    sums_even[...] = jnp.zeros_like(sums_even)
    wb[planes - 1] = jnp.zeros_like(wb[planes - 1])

    @pl.when(jnp.logical_not(has_left))
    def _():
        halo[0] = jnp.zeros_like(halo[0])
        for k in range(views):
            srcs[k, 0] = jnp.zeros_like(srcs[k, 0])

    @pl.when(jnp.logical_not(has_right))
    def _():
        halo[1] = jnp.zeros_like(halo[1])
        for k in range(views):
            srcs[k, 2] = jnp.zeros_like(srcs[k, 2])

    pl.semaphore_wait(barrier, len(partners))
    for k in [0, REF, *range(1, views)]:
        stage1(k)

    lane = iota((rows, 128), 1)

    def pack(w, n, spot):
        first = 12 * spot
        turned = pltpu.roll(jnp.where(lane < 64, w[:, :128], w[:, 128:]), first + 6, 1)
        slab[n] = jnp.where((lane >= first) & (lane < first + 12), turned, slab[n])

    def permute(value):
        return jnp.concatenate(
            [mm(perm[...], value[PART * h : PART * (h + 1)]).astype(BF16) for h in range(halves)], axis=0
        )

    def put_sums(target, n, value):
        wide = value.shape[1]
        cells = value.reshape(halves, RUN, SUB, wide)
        sub = iota((HALF, SUB, wide), 1)
        target[n, :, HALF : HALF + RUN] = cells
        before = [pltpu.roll(cells[h, RUN - HALF :], 1, 1) for h in range(halves)]
        after = [pltpu.roll(cells[h, :HALF], SUB - 1, 1) for h in range(halves)]
        zero = jnp.zeros((HALF, SUB, wide), F32)
        for h in range(halves):
            target[n, h, :HALF] = jnp.where(sub == 0, before[h - 1] if h else zero, before[h])
            target[n, h, HALF + RUN :] = jnp.where(
                sub == SUB - 1, after[h + 1] if h + 1 < halves else zero, after[h]
            )

    def row_sums(source, n, h, first, size, lanes):
        v = source[n, h, first : first + size + 6, :, lanes]
        two = v[: size + 5] + v[1 : size + 6]
        four = two[:size] + two[2 : size + 2]
        return (four + two[4 : size + 4]) + v[6 : size + 6]

    stage2(0)
    stage2(REF)
    stage2(1)
    if views > 2:
        stage2(2)
    stage3(0)
    finish(REF)

    r = permute(ref_all[...].reshape(rows, TW))
    rb[...] = r
    rf = r.astype(F32)
    pack(rf, 0, EDGE_SLOTS)
    rr_hi, rr_lo = split2(rf * rf)
    put_sums(sums_odd, 0, mm(r, band[...]))
    put_sums(sums_odd, 1, mm(rr_hi, band[...]) + mm(rr_lo, band[...]))
    for h in range(halves):
        sr = row_sums(sums_odd, 0, h, 0, RUN, slice(0, TW))
        srr = row_sums(sums_odd, 1, h, 0, RUN, slice(0, TW))
        mean = sr * (1.0 / COUNT)
        rn[h] = mean
        inv[h] = lax.rsqrt(jnp.maximum(srr - sr * mean, 0.0) + STABILIZER)

    STEP = 16

    def bring(v):
        finish(v)
        warp_copy(v).wait()

    def pick(v):
        for b in range(3):
            picked[b] = permute(srcs[v, b].reshape(rows, TW))

    def resample(v, p):
        blocks = [picked[off_ref[p, s, 0, v] + 1] for s in range(4)]
        w = mm(jnp.concatenate(blocks, axis=1), warp[v, p].reshape(4 * TW, TW))
        wb[p] = w.astype(BF16)
        i = v * planes + p
        pack(w, i // EDGE_SLOTS, i % EDGE_SLOTS)

    buffers = (sums_even, sums_odd)

    def box_columns(p):
        target = buffers[p % 2]
        w = wb[p]
        put_sums(target, 0, mm(w, band[...]))
        put_sums(target, 1, mm(w * w, band[...]))
        put_sums(target, 2, mm(w * rb[...], band[...]))

    def correlate(p):
        source = buffers[p % 2]
        for h in range(halves):
            for first in range(0, RUN, STEP):
                for lanes in (slice(0, 128), slice(128, 256)):
                    sw, sww, srw = [row_sums(source, n, h, first, STEP, lanes) for n in range(3)]
                    here = slice(first, first + STEP)
                    covar = srw - rn[h, here, :, lanes] * sw
                    var = jnp.maximum(sww - sw * (sw * (1.0 / COUNT)), 0.0) + STABILIZER
                    acc[p, h, here, :, lanes] += covar * lax.rsqrt(var)

    def view_step(v, carry):
        pl.when(v + 3 < views)(lambda: stage2(v + 3))
        bring(v)
        pick(v)
        for p in range(planes):
            if p == planes // 2:
                stage3(v + 1)
            resample(v, p)
            box_columns((p - 1) % planes)
            correlate((p - 2) % planes)
        return carry

    last = views - 1
    lax.fori_loop(0, last, view_step, 0)
    bring(last)
    pick(last)
    for p in range(planes):
        resample(last, p)
        if p == 0:
            box_columns(planes - 1)
        if p < 2:
            correlate(planes - 2 + p)
    own = jnp.concatenate([slab[n].astype(BF16) for n in range(slabs)], axis=1)
    for g in range(4):
        cells16[g] = mm(own, select[:, 128 * g : 128 * (g + 1)]).astype(BF16)
    for side in (0, 1):
        when_sends(side, lambda side=side: halo_copy(side).start())
    for p in range(planes):
        box_columns(p)
        if p:
            correlate(p - 1)
    correlate(planes - 1)

    for side in (0, 1):
        when_arrives(side, lambda side=side: halo_copy(side).wait_recv())

    edges = []
    for side in (0, 1):
        cells = [halo[0], cells16[0], cells16[1]] if side == 0 else [cells16[2], cells16[3], halo[1]]
        refs = [mm(cell, edge_q[...]).astype(BF16) for cell in cells]
        w, rw = jnp.concatenate(cells, axis=1), jnp.concatenate(refs, axis=1)
        wf, rf = w.astype(F32), rw.astype(F32)

        def summed(value):
            hi, lo = split2(value)
            return mm(hi, edge_t[...]) + mm(lo, edge_t[...])

        put_sums(esums, 0, mm(w, edge_t[...]))
        put_sums(esums, 1, summed(wf * wf))
        put_sums(esums, 2, summed(rf * wf))
        put_sums(esums, 3, mm(rw, edge_t[...]))
        put_sums(esums, 4, summed(rf * rf))
        out = []
        for h in range(halves):
            sw, sww, srw, sr, srr = [row_sums(esums, n, h, 0, RUN, slice(0, 128)) for n in range(5)]
            covar = srw - sr * (sw * (1.0 / COUNT))
            var = jnp.maximum(sww - sw * (sw * (1.0 / COUNT)), 0.0) + STABILIZER
            var_r = jnp.maximum(srr - sr * (sr * (1.0 / COUNT)), 0.0) + STABILIZER
            ncc = covar * (lax.rsqrt(var) * lax.rsqrt(var_r))
            total = ncc
            for v in range(1, views):
                total = total + pltpu.roll(ncc, 128 - 3 * planes * v, 2)
            out.append(total)
        edges.append(out)

    lane3 = iota((RUN, SUB, 128), 2)

    def swap(h, cc):
        return remote(
            low.at[pl.ds(per * h, per), pl.ds(cc, 1)],
            got1.at[pl.ds(per * h, per)],
            p_send.at[h],
            p_recv.at[h],
            (t, sib),
        )

    for h in range(halves):
        for p in range(planes):
            total = acc[p, h] * inv[h]
            l_edge = pltpu.roll(edges[0][h], (128 - 3 * p) % 128, 2)
            r_edge = pltpu.roll(edges[1][h], 125 - 3 * p, 2)
            total = jnp.concatenate(
                [
                    jnp.where(lane3 < 3, l_edge, total[:, :, :128]),
                    jnp.where(lane3 >= 125, r_edge, total[:, :, 128:]),
                ],
                axis=2,
            )
            hi, lo = split2((total * (1.0 / views)).reshape(PART, TW))
            cost = 1.0 - (mm(unperm[...], hi) + mm(unperm[...], lo))
            vol[p, PART * h : PART * (h + 1)] = cost
            cost4 = cost.reshape(per, 2, rows // nq, TW)
            spot = slice(per * h, per * (h + 1))
            low[spot] = cost4 if p == 0 else jnp.minimum(low[spot], cost4)
        swap(h, 1 - c).start()

    def min_copy(xx, way):
        return remote(red.at[xx], got2.at[way - 1], m_send.at[way], m_recv.at[way], (t, 2 * xx + c))

    for h in range(halves):
        swap(h, 1 - c).wait_recv()
        spot = slice(per * h, per * (h + 1))
        red[spot] = jnp.minimum(low[spot, pl.ds(c, 1)], got1[spot])
        for xx in range(per * h, per * (h + 1)):
            pl.when(x != xx)(lambda xx=xx: min_copy(xx, lax.rem(xx - x + nx, nx)).start())
    for d in range(1, nx):
        min_copy(at_x(d), d).wait_recv()
    best = red[x, 0]
    for d in range(1, nx):
        best = jnp.minimum(best, got2[d - 1, 0])
    best_ref[...] = best

    for k in [REF, *range(views)]:
        drain(k)
    for side in (0, 1):
        when_sends(side, lambda side=side: halo_copy(side).wait_send())
    for h in range(halves):
        swap(h, 1 - c).wait_send()
    for d in range(1, nx):
        min_copy(at_x(d), d).wait_send()


def solution(mesh):
    tiles, nq = mesh.shape["tile"], mesh.shape["plane"]
    nx = nq // 2

    def local(reference_image, source_images, warps, offsets):
        views, planes = warps.shape[0], warps.shape[1]
        part = reference_image.shape[0]
        rows = nq * part
        halves = rows // PART
        slabs = -(-views * planes // EDGE_SLOTS)
        vmem = pltpu.VMEM
        dma = pltpu.SemaphoreType.DMA
        scratch = [
            vmem((views, 3, nx, 2, part, TW), BF16),
            vmem((nx, 2, part, TW), BF16),
            vmem((views, planes, 4, TW, TW), BF16),
            vmem((3, rows, TW), BF16),
            vmem((planes, rows, TW), BF16),
            vmem((rows, TW), BF16),
            vmem((3, halves, RUN + 2 * HALF, SUB, TW), F32),
            vmem((3, halves, RUN + 2 * HALF, SUB, TW), F32),
            vmem((planes, halves, RUN, SUB, TW), F32),
            vmem((halves, RUN, SUB, TW), F32),
            vmem((halves, RUN, SUB, TW), F32),
            vmem((slabs, rows, 128), F32),
            vmem((4, rows, 128), BF16),
            vmem((2, rows, 128), BF16),
            vmem((TW, TW), BF16),
            vmem((TW, TW), BF16),
            vmem((TW, TW), BF16),
            vmem((128 * slabs, 512), BF16),
            vmem((384, 128), BF16),
            vmem((128, 128), BF16),
            vmem((5, halves, RUN + 2 * HALF, SUB, 128), F32),
            vmem((nx, 2, part, TW), F32),
            vmem((nx, 1, part, TW), F32),
            vmem((nx, 1, part, TW), F32),
            vmem((nx - 1, 1, part, TW), F32),
            dma((views + 1, nx - 1)),
            dma((views + 1, nx - 1)),
            dma((views + 1,)),
            dma((views, 2)),
            dma((views, 2)),
            dma((views + 1, 3)),
            dma((views + 1, 3)),
            dma((views,)),
            dma((2,)),
            dma((2,)),
            dma((halves,)),
            dma((halves,)),
            dma((nx,)),
            dma((nx,)),
        ]
        far = pl.BlockSpec(memory_space=pltpu.HBM)
        near = pl.BlockSpec(memory_space=pltpu.VMEM)
        return pl.pallas_call(
            functools.partial(body, views, planes, tiles, nq),
            out_shape=(pltpu.VMEM((planes, rows, TW), F32), pltpu.VMEM((part, TW), F32)),
            in_specs=[far, far, far, pl.BlockSpec(memory_space=pltpu.SMEM)],
            out_specs=(near, near),
            scratch_shapes=scratch,
            compiler_params=pltpu.CompilerParams(
                collective_id=0, has_side_effects=True, vmem_limit_bytes=63300 * 1024
            ),
        )(reference_image, source_images, warps, offsets.transpose(1, 2, 3, 0))

    return jax.shard_map(
        local,
        mesh=mesh,
        in_specs=(
            P("plane", "tile"),
            P(None, "plane", "tile"),
            P(None, "plane", None, None, "tile"),
            P(None, "plane", None, "tile"),
        ),
        out_specs=(P("plane", None, "tile"), P("plane", "tile")),
        check_vma=False,
    )
```

time: 78.2 us -> 56.6 us (0.72)
  Pallas kernels: 72.3 us -> 53.8 us
  local copies, waits for them, and re-layouts: 5.13 us -> 1.95 us
    pallas_call x1, Pallas kernels: 72.3 us -> 53.8 us  [local(): pl.pallas_call(functools.partial(body, views, planes, tiles, nq), out_sha...]
    unnamed x5 -> x2, local copies, waits for them, and re-layouts: 4.51 us -> 1.95 us
where the time goes in v2:
time: 56.6 us; the launch traced here: 56.4 us
  Pallas kernels  53.8 us (95%)
  local copies, waits for them, and re-layouts  1.95 us (3%)
  between operations  0.64 us (1%)
    pallas_call x1, Pallas kernels, local(): pl.pallas_call(functools.partial(body, views, planes, tiles, nq), out_sha...  53.8 us
    unnamed x2, local copies, waits for them, and re-layouts  1.95 us

profile of v2, /device:TPU:1, one launch (start us, length us, event | category | flops | bytes accessed | tf_op | source)
XLA Modules:
  0.0 56.4 jit_solution(16671568262969679009)
XLA Ops:
  0.6 53.8 %shard_map.59 = (f32[4,512,256]{2,1,0:T(8,128)S(1)}, f32[64,256]{1,0:T(8,128)S(1)}) custom-call(bf16[64,256]{1,0:T(8,128)(2,1)} %ref_hbm.1, bf16[6,64,256]{2,1,0:T(8,128)(2,1)} %src_hbm.1, bf16[6,4,4,256,256]{4,3,2,1,0:T(8,128)(2,1)} %warp_hbm.1, s32[4,4,1,6]{3,2,1,0:T(1,128)} %bitcast.1), custom_call_target="tpu_custom_call" | custom-call | tf_op jit(solution)/shard_map/pallas_call | solution.py:538
  54.5 1.3 %copy.8 = f32[4,512,256]{2,1,0:T(8,128)} copy(f32[4,512,256]{2,1,0:T(8,128)S(1)} %get-tuple-element.2) | data formatting | bytes 4194304
  55.8 0.6 %copy.9 = f32[64,256]{1,0:T(8,128)} copy(f32[64,256]{1,0:T(8,128)S(1)} %get-tuple-element.3) | data formatting | bytes 131072

commit v3 on v2

--- a/solution.py
+++ b/solution.py
@@ -73,15 +73,21 @@
     edge_t,
     edge_q,
     esums,
+    eparts,
     low,
     got1,
     red,
     got2,
+    emin,
+    egot,
+    etall,
     s1_send,
     s1_recv,
     own_sem,
     z_send,
     z_recv,
+    y_send,
+    y_recv,
     f_send,
     f_recv,
     w_sem,
@@ -91,8 +97,11 @@
     p_recv,
     m_send,
     m_recv,
+    e_send,
+    e_recv,
 ):
     nx = nq // 2
+    zviews = views - views // 3
     rows = nq * ref_hbm.shape[0]
     halves = rows // PART
     per = nx // halves
@@ -159,6 +168,21 @@
             (right if side == 0 else left, q),
         )
 
+    def raw_copy(k, side):
+        return remote(
+            piece(k), slot2(k, side, x), z_send.at[k, side], z_recv.at[k, side], (right if side == 0 else left, q)
+        )
+
+    def slot2(k, side, xx):
+        return srcs.at[k, 2 * side, xx, c]
+
+    def y_copy(k, side, d, where):
+        place = slot2(k, side, where)
+        n = k - zviews
+        return remote(
+            place, place, y_send.at[n, side, d - 1], y_recv.at[n, side, d - 1], (t, 2 * at_x(d) + c)
+        )
+
     def sib_copy(k, block, cc):
         n = sem_at(k)
         place = column(k, block, cc)
@@ -179,16 +203,37 @@
         for d in range(1, nx):
             x_arrival(k, d).wait_recv()
         if k is not REF:
-            for side in (0, 1):
-                when_sends(side, lambda side=side: z_copy(k, side).start())
+
+            @pl.when(k < zviews)
+            def _():
+                for side in (0, 1):
+                    when_sends(side, lambda side=side: z_copy(k, side).start())
+
         sib_copy(k, 1, c).start()
+
+    def pass_on(k):
+        for side in (0, 1):
+
+            @functools.partial(when_arrives, side)
+            def _():
+                raw_copy(k, side).wait_recv()
+                for d in range(1, nx):
+                    y_copy(k, side, d, x).start()
 
     def stage3(k):
         for side in (0, 1):
 
             @functools.partial(when_arrives, side)
             def _():
-                z_copy(k, side).wait_recv()
+                @pl.when(k < zviews)
+                def _():
+                    z_copy(k, side).wait_recv()
+
+                @pl.when(k >= zviews)
+                def _():
+                    for d in range(1, nx):
+                        y_copy(k, side, d, at_x(-d)).wait_recv()
+
                 sib_copy(k, 2 * side, c).start()
 
     def finish(k):
@@ -203,8 +248,12 @@
         sib_copy(k, 1, c).wait_send()
         if k is not REF:
             for side in (0, 1):
-                when_sends(side, lambda side=side: z_copy(k, side).wait_send())
+                late = k >= zviews
+                copy = raw_copy if late else z_copy
+                when_sends(side, lambda side=side, copy=copy: copy(k, side).wait_send())
                 when_arrives(side, lambda side=side: sib_copy(k, 2 * side, c).wait_send())
+                for d in range(1, nx if late else 1):
+                    when_arrives(side, lambda side=side, d=d: y_copy(k, side, d, x).wait_send())
 
     def warp_copy(k):
         return pltpu.make_async_copy(warp_hbm.at[k], warp.at[k], w_sem.at[k])
@@ -220,6 +269,7 @@
 
     barrier = pltpu.get_barrier_semaphore()
     partners = [(t, 2 * at_x(d) + c) for d in range(1, nx)] + [(t, sib), (left, q), (right, q)]
+    partners += [(t, 2 * at_x(d) + 1 - c) for d in range(1, nx)]
     for dev in partners:
         pl.semaphore_signal(barrier, inc=1, device_id=dev, device_id_type=MESH)
     for k in [0, REF, *range(1, views)]:
@@ -264,7 +314,11 @@
             srcs[k, 2] = jnp.zeros_like(srcs[k, 2])
 
     pl.semaphore_wait(barrier, len(partners))
-    for k in [0, REF, *range(1, views)]:
+    stage1(0)
+    for k in range(zviews, views):
+        for side in (0, 1):
+            when_sends(side, lambda side=side, k=k: raw_copy(k, side).start())
+    for k in [REF, *range(1, views)]:
         stage1(k)
 
     lane = iota((rows, 128), 1)
@@ -305,6 +359,8 @@
     if views > 2:
         stage2(2)
     stage3(0)
+    for k in range(zviews, views):
+        pass_on(k)
     finish(REF)
 
     r = permute(ref_all[...].reshape(rows, TW))
@@ -391,28 +447,65 @@
             correlate(p - 1)
     correlate(planes - 1)
 
-    for side in (0, 1):
-        when_arrives(side, lambda side=side: halo_copy(side).wait_recv())
-
-    edges = []
-    for side in (0, 1):
-        cells = [halo[0], cells16[0], cells16[1]] if side == 0 else [cells16[2], cells16[3], halo[1]]
+    def edge_terms(cells, taps):
         refs = [mm(cell, edge_q[...]).astype(BF16) for cell in cells]
         w, rw = jnp.concatenate(cells, axis=1), jnp.concatenate(refs, axis=1)
         wf, rf = w.astype(F32), rw.astype(F32)
 
         def summed(value):
             hi, lo = split2(value)
-            return mm(hi, edge_t[...]) + mm(lo, edge_t[...])
-
-        put_sums(esums, 0, mm(w, edge_t[...]))
-        put_sums(esums, 1, summed(wf * wf))
-        put_sums(esums, 2, summed(rf * wf))
-        put_sums(esums, 3, mm(rw, edge_t[...]))
-        put_sums(esums, 4, summed(rf * rf))
+            return mm(hi, taps) + mm(lo, taps)
+
+        return [mm(w, taps), summed(wf * wf), summed(rf * wf), mm(rw, taps), summed(rf * rf)]
+
+    for side in (0, 1):
+        taps = edge_t[128:] if side == 0 else edge_t[:256]
+        for n, term in enumerate(edge_terms([cells16[2 * side], cells16[2 * side + 1]], taps)):
+            eparts[side, n] = term
+
+    def in_order(value):
+        hi, lo = split2(value * (1.0 / views))
+        return 1.0 - (mm(unperm[...], hi) + mm(unperm[...], lo))
+
+    for h in range(halves):
+        for p in range(planes):
+            cost = in_order((acc[p, h] * inv[h]).reshape(PART, TW))
+            vol[p, PART * h : PART * (h + 1)] = cost
+            cost4 = cost.reshape(per, 2, rows // nq, TW)
+            spot = slice(per * h, per * (h + 1))
+            low[spot] = cost4 if p == 0 else jnp.minimum(low[spot], cost4)
+
+    def swap(h, cc):
+        return remote(
+            low.at[pl.ds(per * h, per), pl.ds(cc, 1)],
+            got1.at[pl.ds(per * h, per)],
+            p_send.at[h],
+            p_recv.at[h],
+            (t, sib),
+        )
+
+    def min_copy(xx, way):
+        return remote(red.at[xx], got2.at[way - 1], m_send.at[way], m_recv.at[way], (t, 2 * xx + c))
+
+    for h in range(halves):
+        swap(h, 1 - c).start()
+
+    for side in (0, 1):
+        when_arrives(side, lambda side=side: halo_copy(side).wait_recv())
+    for h in range(halves):
+        swap(h, 1 - c).wait_recv()
+    red[...] = jnp.minimum(low[:, pl.ds(c, 1)], got1[...])
+    for d in range(1, nx):
+        min_copy(at_x(d), d).start()
+
+    edges = []
+    for side in (0, 1):
+        taps = edge_t[:128] if side == 0 else edge_t[256:]
+        for n, term in enumerate(edge_terms([halo[side]], taps)):
+            put_sums(esums.at[side], n, eparts[side, n] + term)
         out = []
         for h in range(halves):
-            sw, sww, srw, sr, srr = [row_sums(esums, n, h, 0, RUN, slice(0, 128)) for n in range(5)]
+            sw, sww, srw, sr, srr = [row_sums(esums.at[side], n, h, 0, RUN, slice(0, 128)) for n in range(5)]
             covar = srw - sr * (sw * (1.0 / COUNT))
             var = jnp.maximum(sww - sw * (sw * (1.0 / COUNT)), 0.0) + STABILIZER
             var_r = jnp.maximum(srr - sr * (sr * (1.0 / COUNT)), 0.0) + STABILIZER
@@ -420,55 +513,47 @@
             total = ncc
             for v in range(1, views):
                 total = total + pltpu.roll(ncc, 128 - 3 * planes * v, 2)
-            out.append(total)
+            out.append(in_order(total.reshape(PART, 128)))
         edges.append(out)
 
-    lane3 = iota((RUN, SUB, 128), 2)
-
-    def swap(h, cc):
+    lane2 = iota((PART, 128), 1)
+    chip = rows // nx
+    for h in range(halves):
+        here = slice(PART * h, PART * (h + 1))
+        both = []
+        for side in (0, 1):
+            least = None
+            for p in range(planes):
+                turned = pltpu.roll(edges[side][h], 125 - 3 * p if side else (128 - 3 * p) % 128, 1)
+                least = turned if least is None else jnp.minimum(least, turned)
+            both.append(least)
+        sides = pltpu.roll(jnp.where(lane2 < 64, both[0], both[1]), 3, 1)
+        flat = sides.T
+        for n in range(per):
+            emin[per * h + n] = flat[:SUB, chip * n : chip * (n + 1)]
+
+    def side_copy(dx, dc):
+        n = 2 * dx + dc - 1
         return remote(
-            low.at[pl.ds(per * h, per), pl.ds(cc, 1)],
-            got1.at[pl.ds(per * h, per)],
-            p_send.at[h],
-            p_recv.at[h],
-            (t, sib),
-        )
+            emin.at[at_x(dx)],
+            egot.at[n],
+            e_send.at[n],
+            e_recv.at[n],
+            (t, 2 * at_x(dx) + (1 - c if dc else c)),
+        )
+
+    others = [(dx, dc) for dx in range(nx) for dc in (0, 1) if dx or dc]
+    for dx, dc in others:
+        side_copy(dx, dc).start()
 
     for h in range(halves):
-        for p in range(planes):
-            total = acc[p, h] * inv[h]
-            l_edge = pltpu.roll(edges[0][h], (128 - 3 * p) % 128, 2)
-            r_edge = pltpu.roll(edges[1][h], 125 - 3 * p, 2)
-            total = jnp.concatenate(
-                [
-                    jnp.where(lane3 < 3, l_edge, total[:, :, :128]),
-                    jnp.where(lane3 >= 125, r_edge, total[:, :, 128:]),
-                ],
-                axis=2,
-            )
-            hi, lo = split2((total * (1.0 / views)).reshape(PART, TW))
-            cost = 1.0 - (mm(unperm[...], hi) + mm(unperm[...], lo))
-            vol[p, PART * h : PART * (h + 1)] = cost
-            cost4 = cost.reshape(per, 2, rows // nq, TW)
-            spot = slice(per * h, per * (h + 1))
-            low[spot] = cost4 if p == 0 else jnp.minimum(low[spot], cost4)
-        swap(h, 1 - c).start()
-
-    def min_copy(xx, way):
-        return remote(red.at[xx], got2.at[way - 1], m_send.at[way], m_recv.at[way], (t, 2 * xx + c))
-
-    for h in range(halves):
-        swap(h, 1 - c).wait_recv()
-        spot = slice(per * h, per * (h + 1))
-        red[spot] = jnp.minimum(low[spot, pl.ds(c, 1)], got1[spot])
-        for xx in range(per * h, per * (h + 1)):
-            pl.when(x != xx)(lambda xx=xx: min_copy(xx, lax.rem(xx - x + nx, nx)).start())
-    for d in range(1, nx):
-        min_copy(at_x(d), d).wait_recv()
-    best = red[x, 0]
-    for d in range(1, nx):
-        best = jnp.minimum(best, got2[d - 1, 0])
-    best_ref[...] = best
+        here = slice(PART * h, PART * (h + 1))
+        for side in (0, 1):
+            lanes = slice(128 * side, 128 * (side + 1))
+            inside = (lane2 >= 125) if side else (lane2 < 3)
+            for p in range(planes):
+                turned = pltpu.roll(edges[side][h], 125 - 3 * p if side else (128 - 3 * p) % 128, 1)
+                vol[p, here, lanes] = jnp.where(inside, turned, vol[p, here, lanes])
 
     for k in [REF, *range(views)]:
         drain(k)
@@ -476,8 +561,28 @@
         when_sends(side, lambda side=side: halo_copy(side).wait_send())
     for h in range(halves):
         swap(h, 1 - c).wait_send()
+
+    for d in range(1, nx):
+        min_copy(at_x(d), d).wait_recv()
+    best = red[x, 0]
+    for d in range(1, nx):
+        best = jnp.minimum(best, got2[d - 1, 0])
+    least = emin[x]
+    for dx, dc in others:
+        side_copy(dx, dc).wait_recv()
+    for dx, dc in others:
+        least = jnp.minimum(least, egot[2 * dx + dc - 1])
+    part = rows // nq
+    etall[...] = jnp.concatenate([least, jnp.zeros((128 - SUB, chip), F32)], axis=0).T
+    sides = etall[pl.ds(pl.multiple_of(c * part, part), part)]
+    lane1 = iota((part, 128), 1)
+    best_ref[:, :128] = jnp.where(lane1 < 3, pltpu.roll(sides, 125, 1), best[:, :128])
+    best_ref[:, 128:] = jnp.where(lane1 >= 125, pltpu.roll(sides, 125, 1), best[:, 128:])
+
     for d in range(1, nx):
         min_copy(at_x(d), d).wait_send()
+    for dx, dc in others:
+        side_copy(dx, dc).wait_send()
 
 
 def solution(mesh):
@@ -513,16 +618,22 @@
             vmem((128 * slabs, 512), BF16),
             vmem((384, 128), BF16),
             vmem((128, 128), BF16),
-            vmem((5, halves, RUN + 2 * HALF, SUB, 128), F32),
+            vmem((2, 5, halves, RUN + 2 * HALF, SUB, 128), F32),
+            vmem((2, 5, rows, 128), F32),
             vmem((nx, 2, part, TW), F32),
             vmem((nx, 1, part, TW), F32),
             vmem((nx, 1, part, TW), F32),
             vmem((nx - 1, 1, part, TW), F32),
+            vmem((nx, SUB, 2 * part), F32),
+            vmem((nq - 1, SUB, 2 * part), F32),
+            vmem((2 * part, 128), F32),
             dma((views + 1, nx - 1)),
             dma((views + 1, nx - 1)),
             dma((views + 1,)),
             dma((views, 2)),
             dma((views, 2)),
+            dma((views // 3, 2, nx - 1)),
+            dma((views // 3, 2, nx - 1)),
             dma((views + 1, 3)),
             dma((views + 1, 3)),
             dma((views,)),
@@ -532,6 +643,8 @@
             dma((halves,)),
             dma((nx,)),
             dma((nx,)),
+            dma((nq - 1,)),
+            dma((nq - 1,)),
         ]
         far = pl.BlockSpec(memory_space=pltpu.HBM)
         near = pl.BlockSpec(memory_space=pltpu.VMEM)

time: 56.6 us -> 54 us (0.954)
  Pallas kernels: 53.8 us -> 51.3 us
    pallas_call x1, Pallas kernels: 53.8 us -> 51.3 us  [local(): pl.pallas_call(functools.partial(body, views, planes, tiles, nq), out_sha...]
where the time goes in v3:
time: 54 us; the launch traced here: 53.9 us
  Pallas kernels  51.3 us (95%)
  local copies, waits for them, and re-layouts  1.95 us (4%)
  between operations  0.64 us (1%)
    pallas_call x1, Pallas kernels, local(): pl.pallas_call(functools.partial(body, views, planes, tiles, nq), out_sha...  51.3 us
    unnamed x2, local copies, waits for them, and re-layouts  1.95 us

profile of v3, /device:TPU:1, one launch (start us, length us, event | category | flops | bytes accessed | tf_op | source)
XLA Modules:
  0.0 53.9 jit_solution(912780379633283711)
XLA Ops:
  0.6 51.3 %shard_map.59 = (f32[4,512,256]{2,1,0:T(8,128)S(1)}, f32[64,256]{1,0:T(8,128)S(1)}) custom-call(bf16[64,256]{1,0:T(8,128)(2,1)} %ref_hbm.1, bf16[6,64,256]{2,1,0:T(8,128)(2,1)} %src_hbm.1, bf16[6,4,4,256,256]{4,3,2,1,0:T(8,128)(2,1)} %warp_hbm.1, s32[4,4,1,6]{3,2,1,0:T(1,128)} %bitcast.1), custom_call_target="tpu_custom_call" | custom-call | tf_op jit(solution)/shard_map/pallas_call | solution.py:651
  51.9 1.3 %copy.8 = f32[4,512,256]{2,1,0:T(8,128)} copy(f32[4,512,256]{2,1,0:T(8,128)S(1)} %get-tuple-element.2) | data formatting | bytes 4194304
  53.2 0.6 %copy.9 = f32[64,256]{1,0:T(8,128)} copy(f32[64,256]{1,0:T(8,128)S(1)} %get-tuple-element.3) | data formatting | bytes 131072

commit v4 on v3

--- a/solution.py
+++ b/solution.py
@@ -101,7 +101,7 @@
     e_recv,
 ):
     nx = nq // 2
-    zviews = views - views // 3
+    zviews = views - views // 6
     rows = nq * ref_hbm.shape[0]
     halves = rows // PART
     per = nx // halves
@@ -632,8 +632,8 @@
             dma((views + 1,)),
             dma((views, 2)),
             dma((views, 2)),
-            dma((views // 3, 2, nx - 1)),
-            dma((views // 3, 2, nx - 1)),
+            dma((views // 6, 2, nx - 1)),
+            dma((views // 6, 2, nx - 1)),
             dma((views + 1, 3)),
             dma((views + 1, 3)),
             dma((views,)),

time: 54 us -> 53.9 us (level)
  no operation moved by 1% of the time
where the time goes in v4:
time: 53.9 us; the launch traced here: 53.8 us
  Pallas kernels  51.2 us (95%)
  local copies, waits for them, and re-layouts  1.95 us (4%)
  between operations  0.64 us (1%)
    pallas_call x1, Pallas kernels, local(): pl.pallas_call(functools.partial(body, views, planes, tiles, nq), out_sha...  51.2 us
    unnamed x2, local copies, waits for them, and re-layouts  1.95 us

profile of v4, /device:TPU:1, one launch (start us, length us, event | category | flops | bytes accessed | tf_op | source)
XLA Modules:
  0.0 53.8 jit_solution(4882081810623076025)
XLA Ops:
  0.6 51.2 %shard_map.59 = (f32[4,512,256]{2,1,0:T(8,128)S(1)}, f32[64,256]{1,0:T(8,128)S(1)}) custom-call(bf16[64,256]{1,0:T(8,128)(2,1)} %ref_hbm.1, bf16[6,64,256]{2,1,0:T(8,128)(2,1)} %src_hbm.1, bf16[6,4,4,256,256]{4,3,2,1,0:T(8,128)(2,1)} %warp_hbm.1, s32[4,4,1,6]{3,2,1,0:T(1,128)} %bitcast.1), custom_call_target="tpu_custom_call" | custom-call | tf_op jit(solution)/shard_map/pallas_call | solution.py:651
  51.8 1.3 %copy.8 = f32[4,512,256]{2,1,0:T(8,128)} copy(f32[4,512,256]{2,1,0:T(8,128)S(1)} %get-tuple-element.2) | data formatting | bytes 4194304
  53.2 0.6 %copy.9 = f32[64,256]{1,0:T(8,128)} copy(f32[64,256]{1,0:T(8,128)S(1)} %get-tuple-element.3) | data formatting | bytes 131072
